TPU v7x, 512 devices: a whole 4x4x16 slice. The times are simulated.
512 devices in a mesh: span: 16 (over z), seq: 32 (over y, x, core).
Axes of the slice: x: 4, y: 4, z: 16, core: 2. Of those that a mesh axis runs over, the one named last changes fastest.
Arguments:
- latents: bfloat16 [4096, 6144], P(('span', 'seq')), may hold values from -6 to 6
- levels: int32 [16], P('span'), may hold values from 0 to 15
- order: int32 [16], replicated, may hold values from 0 to 15, each once
- level_table: float32 [16, 12288], replicated, may hold values from -2 to 7, as said below
- q_gain: float32 [128], replicated, may hold values from 0.5 to 2.5
- k_gain: float32 [128], replicated, may hold values from 0.5 to 2.5
- w_qkv: bfloat16 [6144, 12288], P('span', 'seq'), may hold values from -0.078125 to 0.078125
- w_out: bfloat16 [4096, 6144], P('seq', 'span'), may hold values from -0.09375 to 0.09375
Outputs:
- mixed: bfloat16 [4096, 6144], P(('span', 'seq'))
Inputs may be any that keep to these rules, and one draw needn't show every extreme that they name: Span j lies before span i when order[j] < order[i]; each span attends to itself and to the spans before it. `level_table`: the shift entries lie within -2 and 2 and every scale entry is above -1.
All inputs are finite; a program needn't handle non-finite values.
Results may differ from a plain program's by a relative error of at most 0.02.
Values may be sent and summed in bfloat16 or wider, within the bound.
A program may use at most 64 MiB of HBM per device.

v0:
```python
import jax
import jax.numpy as jnp
from jax import lax
from jax.sharding import PartitionSpec as P

HD = 128


def modulate(latents, shift, scale):
    values = latents.astype(jnp.float32)
    center = values - jnp.mean(values, axis=1, keepdims=True)
    spread = jnp.mean(center * center, axis=1, keepdims=True)
    return (center * lax.rsqrt(spread + 1e-06) * (1.0 + scale) + shift).astype(jnp.bfloat16)


def head_norm(block, gain):
    values = block.astype(jnp.float32)
    square = jnp.mean(values * values, axis=-1, keepdims=True)
    return (values * lax.rsqrt(square + 1e-06) * gain).astype(jnp.bfloat16)


def orders_of(count, span_len, order):
    span_ids = jnp.arange(order.shape[0], dtype=jnp.int32)
    key_span = jnp.arange(count, dtype=jnp.int32) // span_len
    return jnp.sum(jnp.where(key_span[:, None] == span_ids[None, :], order[None, :], 0), axis=1)


def accumulate(queries, key_piece, val_piece, allowed):
    scores = jnp.einsum(
        "qhe,khe->hqk", queries, key_piece, preferred_element_type=jnp.float32
    ) * HD ** (-0.5)
    probs = jnp.where(allowed[None, None, :], jnp.exp(scores), 0.0)
    row_total = jnp.sum(probs, axis=2)
    weighted = jnp.einsum(
        "hqk,khe->hqe", probs.astype(jnp.bfloat16), val_piece, preferred_element_type=jnp.float32
    )
    return (row_total, weighted)


def finish(state):
    row_total, weighted_sum = state
    return jnp.transpose((weighted_sum / row_total[:, :, None]).astype(jnp.bfloat16), (1, 0, 2))


def body(latents, levels, order, level_table, q_gain, k_gain, w_qkv, w_out):
    width = latents.shape[1]
    level_row = lax.dynamic_index_in_dim(level_table, levels[0], 0, keepdims=False)
    shift = level_row[None, :width]
    scale = level_row[None, width:]
    gathered = lax.all_gather(latents, "seq", axis=0, tiled=True)
    modulated = modulate(gathered, shift, scale)
    span_len = modulated.shape[0]
    qkv = jnp.dot(
        modulated,
        lax.all_gather(w_qkv, "span", axis=0, tiled=True),
        preferred_element_type=jnp.float32,
    )
    heads_here = w_qkv.shape[1] // (3 * HD)
    qkv = qkv.astype(jnp.bfloat16).reshape(span_len, heads_here, 3, HD)
    query = head_norm(qkv[:, :, 0], q_gain)
    keys = head_norm(qkv[:, :, 1], k_gain)
    vals = qkv[:, :, 2]
    span_ids = jnp.arange(order.shape[0], dtype=jnp.int32)
    own_order = jnp.sum(jnp.where(span_ids == lax.axis_index("span"), order, 0))
    key_piece = lax.all_gather(keys, "span", axis=0, tiled=True)
    val_piece = lax.all_gather(vals, "span", axis=0, tiled=True)
    key_order = orders_of(key_piece.shape[0], span_len, order)
    states = accumulate(query, key_piece, val_piece, key_order <= own_order)
    rows_out = finish(states)
    attn = rows_out.reshape(span_len, heads_here * HD)
    terms = jnp.dot(
        attn, lax.all_gather(w_out, "span", axis=1, tiled=True), preferred_element_type=jnp.float32
    )
    return lax.psum_scatter(terms.astype(jnp.bfloat16), "seq", scatter_dimension=0, tiled=True)


def solution(mesh):
    placed = (
        P(("span", "seq"), None),
        P("span"),
        P(),
        P(),
        P(),
        P(),
        P("span", "seq"),
        P("seq", "span"),
    )
    return jax.shard_map(
        body, mesh=mesh, in_specs=placed, out_specs=P(("span", "seq"), None), check_vma=False
    )
```

profile of v0, /device:TPU:1, one launch (start us, length us, event | category | flops | bytes accessed | tf_op | source)
XLA Modules:
  0.0 483.3 jit_solution(11525285236629363089)
XLA Ops:
  6.5 0.0 all-gather.7.cloned.1.call-start
  6.5 0.7 all-gather.7.cloned.1.call-update
  7.3 0.0 all-gather.9.cloned.1.call-start
  7.3 0.7 all-gather.9.cloned.1.call-update
  8.0 0.0 all-gather.11.cloned.1.call-start
  8.7 1.2 dynamic-slice_add_fusion
  9.9 66.8 %all-gather.7.cloned.1.call-done = bf16[256,6144]{1,0:T(8,128)(2,1)} async-done(((bf16[8,6144]{1,0:T(8,128)(2,1)}), bf16[256,6144]{1,0:T(8,128)(2,1)}) %all-gather.7.cloned.1.call-update) | async-done | bytes 3145744 | tf_op jit(solution)/shard_map/all_gather | solution.py:50
  76.7 0.0 copy-start
  76.7 2.5 convert_reduce_fusion
  79.2 0.3 copy-done
  79.5 1.0 fusion.2
  80.5 69.4 %all-gather.9.cloned.1.call-done = bf16[6144,384]{1,0:T(8,128)(2,1)} async-done(((bf16[384,384]{1,0:T(8,128)(2,1)}), bf16[6144,384]{1,0:T(8,128)(2,1)}) %all-gather.9.cloned.1.call-update) | async-done | bytes 4718608 | tf_op jit(solution)/shard_map/all_gather | solution.py:55
  149.9 0.0 copy-start.1
  149.9 0.0 copy-start.2
  149.9 0.0 copy-start.3
  149.9 4.3 fusion.16
  154.3 0.1 copy.12
  154.5 0.0 copy-done.1
  154.5 0.7 fusion.35
  155.2 0.0 all-gather.11.cloned.1.call-update
  155.2 0.0 all-gather.13.cloned.1.call-start
  155.3 0.5 all-gather.13.cloned.1.call-update
  155.8 0.0 all-gather.15.cloned.1.call-start
  155.8 0.6 slice.24
  156.5 0.0 all-gather.15.cloned.1.call-update
  156.5 0.0 reduce-scatter.2.cloned.1.call-start
  156.6 0.0 copy-done.2
  156.6 0.7 fusion.45
  157.3 0.1 select_reduce_fusion
  157.4 0.7 broadcast_compare_fusion
  158.1 62.0 %all-gather.11.cloned.1.call-done = bf16[4096,1,128]{0,2,1:T(8,128)(2,1)} async-done(((bf16[256,1,128]{0,2,1:T(8,128)(2,1)}), bf16[4096,1,128]{0,2,1:T(8,128)(2,1)}) %all-gather.11.cloned.1.call-update) | async-done | bytes 1048592 | tf_op jit(solution)/shard_map/all_gather | solution.py:65
  220.1 0.0 copy-done.3
  220.2 2.5 fusion.46
  222.7 68.8 %all-gather.13.cloned.1.call-done = bf16[128,6144]{1,0:T(8,128)(2,1)} async-done(((bf16[128,384]{1,0:T(8,128)(2,1)}), bf16[128,6144]{1,0:T(8,128)(2,1)}) %all-gather.13.cloned.1.call-update) | async-done | bytes 1572880 | tf_op jit(solution)/shard_map/all_gather | solution.py:72
  291.5 69.8 %all-gather.15.cloned.1.call-done = bf16[4096,1,1,128]{0,3,2,1:T(8,128)(2,1)} async-done(((bf16[256,1,1,128]{0,3,2,1:T(8,128)(2,1)}), bf16[4096,1,1,128]{0,3,2,1:T(8,128)(2,1)}) %all-gather.15.cloned.1.call-update) | async-done | bytes 1048592 | tf_op jit(solution)/shard_map/all_gather | solution.py:66
  361.3 6.1 %convolution_convert_fusion = bf16[256,6144]{1,0:T(8,128)(2,1)} fusion(bf16[128,6144]{1,0:T(8,128)(2,1)} %all-gather.13.cloned.1.call-done, bf16[256,4096]{1,0:T(8,128)(2,1)S(1)} %get-tuple-element.8, bf16[4096,1,1,128]{0,3,2,1:T(8,128)(2,1)} %all-gather.15.cloned.1.call-done, f32[256]{0:T(256)S(1)} %get-tuple-element.7), kind=kOutput, calls=%fused_computation.2 | convolution fusion | flops 672727040 | bytes 7865344 | tf_op jit(solution)/shard_map/dot_general | solution.py:71
  367.3 0.0 reduce-scatter.2.cloned.1.call-update
  367.4 109.1 %reduce-scatter.2.cloned.1.call-done = bf16[8,6144]{1,0:T(8,128)(2,1)} async-done(((bf16[256,6144]{1,0:T(8,128)(2,1)}), bf16[8,6144]{1,0:T(8,128)(2,1)}) %reduce-scatter.2.cloned.1.call-update) | async-done | bytes 98320 | tf_op jit(solution)/shard_map/reduce_scatter | solution.py:74
  (7 shorter events, 0.1 us)
Async XLA Ops:
  6.5 70.1 %all-gather.7.cloned.1.call-start = ((), (), s32[]{:S(2)}) async-start(), calls=%async_computation.1 | async-start | bytes 3244032 | tf_op jit(solution)/shard_map/all_gather | solution.py:50
  7.3 142.7 %all-gather.9.cloned.1.call-start = ((), (), s32[]{:S(2)}) async-start(), calls=%async_computation.2 | async-start | bytes 5013504 | tf_op jit(solution)/shard_map/all_gather | solution.py:55
  8.0 212.1 %all-gather.11.cloned.1.call-start = ((), (), s32[]{:S(2)}) async-start(), calls=%async_computation.3 | async-start | bytes 1114112 | tf_op jit(solution)/shard_map/all_gather | solution.py:65
  76.7 2.8 copy-start
  149.9 4.6 copy-start.1
  149.9 6.6 %copy-start.2 = (s32[16]{0:T(128)S(1)}, s32[16]{0:T(128)}, u32[]{:S(2)}) copy-start(s32[16]{0:T(128)} %param.10) | copy-start | bytes 196
  149.9 70.2 %copy-start.3 = (f32[128]{0:T(128)S(1)}, f32[128]{0:T(128)}, u32[]{:S(2)}) copy-start(f32[128]{0:T(128)} %param.12) | copy-start | bytes 1540
  155.2 136.3 %all-gather.13.cloned.1.call-start = ((), (), s32[]{:S(2)}) async-start(), calls=%async_computation.4 | async-start | bytes 1671168 | tf_op jit(solution)/shard_map/all_gather | solution.py:72
  155.8 205.5 %all-gather.15.cloned.1.call-start = ((), (), s32[]{:S(2)}) async-start(), calls=%async_computation.6 | async-start | bytes 1114112 | tf_op jit(solution)/shard_map/all_gather | solution.py:66
  156.5 320.0 %reduce-scatter.2.cloned.1.call-start = ((), (), s32[]{:S(2)}) async-start(), calls=%async_computation.5 | async-start | bytes 3244032 | tf_op jit(solution)/shard_map/reduce_scatter | solution.py:74
Sparse Core Ops, SparseCore 0:
  10.5 66.1 all-gather.6
  78.8 71.1 all-gather.8
  155.3 64.7 all-gather.10
  222.1 69.3 all-gather.12
  293.3 67.8 all-gather.14
  367.5 108.9 reduce-scatter.1
where the time goes:
time: 484 us; the launch traced here: 483 us
  waiting for transfers between devices  448 us (93%)
  between operations  14.2 us (3%)
  matrix products  12.9 us (3%)
  other arithmetic  6.99 us (1%)
    reduce_scatter x1, waiting for transfers between devices, body(): lax.psum_scatter(terms.astype(jnp.bfloat16), 'seq', scatter_dimension=0,...  109 us
    all_gather x1, waiting for transfers between devices, body(): val_piece = lax.all_gather(vals, 'span', axis=0, tiled=True)  69.8 us
    all_gather x1, waiting for transfers between devices, body(): lax.all_gather(w_qkv, 'span', axis=0, tiled=True)  69.4 us
    all_gather x1, waiting for transfers between devices, body(): lax.all_gather(w_out, 'span', axis=1, tiled=True)  68.8 us
    all_gather x1, waiting for transfers between devices, body(): gathered = lax.all_gather(latents, 'seq', axis=0, tiled=True)  66.8 us
    all_gather x1, waiting for transfers between devices, body(): key_piece = lax.all_gather(keys, 'span', axis=0, tiled=True)  62 us
  transfers between devices with their start and end apart: 6, of which 6 were waited for; matrix products, arithmetic and copies ran while one was open for 2% of the time, Pallas kernels for 0%

commit v1 on v0

v1 whole, which is shorter than its diff:
```python
import jax
import jax.numpy as jnp
from jax import lax
from jax.experimental import pallas as pl
from jax.experimental.pallas import tpu as pltpu
from jax.sharding import PartitionSpec as P

HD = 128
NZ = 16
BF = jnp.bfloat16
F32 = jnp.float32
MESH = pl.DeviceIdType.MESH
BLK = 384
NT = 256
HALF = 128
FAR_FIRST = (8, 7, 9, 6, 10, 5, 11, 4, 12, 3, 13, 2, 14, 1, 15)
AHEAD = 3


def dot(a, b):
    return jnp.dot(a, b, preferred_element_type=F32)


class PlaneGather:
    def __init__(self, buf, rows, x, y, at, s1, s2, rs):
        self.buf, self.rows, self.x, self.y, self.at = buf, rows, x, y, at
        self.s1, self.s2, self.rs = s1, s2, rs
        self.mine = y * 4 + x

    def part(self, block, half):
        return self.buf.at[block, pl.ds(half * self.rows, self.rows)]

    def target(self, half, phase, o):
        along_x = (half == 0) == (phase == 1)
        if along_x:
            return self.at((self.x + o) % 4, self.y)
        return self.at(self.x, (self.y + o) % 4)

    def copy(self, block, half, phase, i, slot=None):
        o = (1, 3, 2)[i]
        sem = self.s1.at[half, i] if phase == 1 else self.s2.at[half, slot, i]
        ref = self.part(block, half)
        return pltpu.make_async_remote_copy(
            src_ref=ref,
            dst_ref=ref,
            send_sem=sem,
            recv_sem=self.rs.at[half, block],
            device_id=self.target(half, phase, o),
            device_id_type=MESH,
        )

    def first(self):
        for i in range(3):
            for half in range(2):
                self.copy(self.mine, half, 1, i).start()

    def wait_block(self, block, half):
        self.copy(block, half, 1, 0).wait_recv()

    def second(self, block):
        by, bx = block // 4, block % 4
        for half in range(2):
            same = (by == self.y) if half == 0 else (bx == self.x)
            slot = bx if half == 0 else by

            @pl.when(same)
            def _(half=half, slot=slot):
                @pl.when(block != self.mine)
                def _():
                    self.wait_block(block, half)

                for i in range(3):
                    self.copy(block, half, 2, i, slot).start()

    def use(self, block):
        by, bx = block // 4, block % 4

        @pl.when(by != self.y)
        def _():
            self.wait_block(block, 0)

        @pl.when(bx != self.x)
        def _():
            self.wait_block(block, 1)

    def drain(self):
        for half in range(2):
            for i in range(3):
                self.copy(self.mine, half, 1, i).wait_send()
                for slot in range(4):
                    self.copy(self.mine, half, 2, i, slot).wait_send()


def kernel(
    lat_ref, lev_ref, ord_ref, tab_ref, qg_ref, kg_ref, w_ref, wo_ref, out_ref,
    wall, woall, xsend, xr, xin, part, cws, cwr, mask,
    qs, ks, vs, nsend, nrecv, dsend, drecv, ag, acc, sibs, sibr, osend, orecv,
    load_sem, xa_s, xa_r, sib_s, sib_r, w1, w2, wr, o1, o2, orr,
    rs_s, rs_r, qkv_s, qkv_r, nd_s, nd_r, ag_s, ag_r, oa_s, oa_r,
):
    z = lax.axis_index("span")
    s = lax.axis_index("seq")
    core = s % 2
    chip = s // 2
    x = chip % 4
    y = chip // 4

    def at(px, py):
        return (z, (py * 4 + px) * 2 + core)

    def along_z(o):
        return ((z + o) % NZ, s)

    sibling = (z, chip * 2 + 1 - core)

    load_w = pltpu.make_async_copy(w_ref, wall.at[chip], load_sem.at[0])
    load_o = pltpu.make_async_copy(wo_ref, woall.at[chip], load_sem.at[1])
    load_w.start()
    load_o.start()

    barrier = pltpu.get_barrier_semaphore()
    for o in FAR_FIRST:
        pl.semaphore_signal(barrier, inc=1, device_id=along_z(o), device_id_type=MESH)
    for o in (2, 1, 3):
        pl.semaphore_signal(barrier, inc=1, device_id=at((x + o) % 4, y), device_id_type=MESH)
        pl.semaphore_signal(barrier, inc=1, device_id=at(x, (y + o) % 4), device_id_type=MESH)
    pl.semaphore_signal(barrier, inc=1, device_id=sibling, device_id_type=MESH)

    width = lat_ref.shape[1]
    level = lev_ref[0]
    row = tab_ref[pl.ds(level, 1), :]
    values = lat_ref[...].astype(F32)
    center = values - jnp.mean(values, axis=1, keepdims=True)
    spread = jnp.mean(center * center, axis=1, keepdims=True)
    modulated = center * lax.rsqrt(spread + 1e-06) * (1.0 + row[:, width:]) + row[:, :width]
    modulated = modulated.astype(BF)
    for j in range(NZ):
        xsend[j] = modulated[:, j * BLK:(j + 1) * BLK]
    xr[core, z] = xsend[z]

    gw = PlaneGather(wall, BLK // 2, x, y, at, w1, w2, wr)
    go = PlaneGather(woall, HD // 2, x, y, at, o1, o2, orr)

    def x_copy(o):
        return pltpu.make_async_remote_copy(
            src_ref=xsend.at[(z + o) % NZ], dst_ref=xr.at[core, z],
            send_sem=xa_s.at[o], recv_sem=xa_r.at[o],
            device_id=along_z(o), device_id_type=MESH,
        )

    def x_arrival(o):
        return pltpu.make_async_remote_copy(
            src_ref=xsend.at[z], dst_ref=xr.at[core, (z + NZ - o) % NZ],
            send_sem=xa_s.at[o], recv_sem=xa_r.at[o],
            device_id=along_z(o), device_id_type=MESH,
        )

    load_w.wait()
    load_o.wait()
    pl.semaphore_wait(barrier, 22)
    for o in FAR_FIRST:
        x_copy(o).start()
    gw.first()

    key_span = (lax.broadcasted_iota(jnp.int32, (NT, HD), 0) % HALF) // 8
    query_span = (lax.broadcasted_iota(jnp.int32, (8, NT), 1) % HALF) // 8
    key_order = jnp.zeros((NT, HD), jnp.int32)
    query_order = jnp.zeros((8, NT), jnp.int32)
    for j in range(NZ):
        place = ord_ref[j]
        key_order = jnp.where(key_span == j, place, key_order)
        query_order = jnp.where(query_span == j, place, query_order)
    key_order = jnp.concatenate([key_order, key_order], axis=1)
    mask[...] = jnp.where(key_order <= query_order[0:1, :], 1.0, 0.0)

    for o in reversed(FAR_FIRST):
        x_arrival(o).wait_recv()

    def x_sib(slot):
        return pltpu.make_async_remote_copy(
            src_ref=xr.at[slot], dst_ref=xr.at[slot],
            send_sem=sib_s.at[0], recv_sem=sib_r.at[0],
            device_id=sibling, device_id_type=MESH,
        )

    x_sib(core).start()

    def place_of(t, way):
        return (z + 8 - t) % NZ if way == 0 else (z + 8 + t) % NZ

    def issue(t):
        gw.second(place_of(t, 0))
        if 0 < t < 8:
            gw.second(place_of(t, 1))

    for t in range(AHEAD):
        issue(t)

    x_sib(1 - core).wait_recv()
    xin[...] = xr[...].astype(F32).reshape(NT, BLK).astype(BF)

    def rs_copy(way, t, p):
        rows = pl.ds(p * HALF, HALF)
        return pltpu.make_async_remote_copy(
            src_ref=cws.at[way, t, rows], dst_ref=cwr.at[way, t, rows],
            send_sem=rs_s.at[way, t, p], recv_sem=rs_r.at[way, t, p],
            device_id=along_z(1 if way == 0 else NZ - 1), device_id_type=MESH,
        )

    for t in range(8):
        if t == 0:
            block = place_of(0, 0)
            gw.use(block)
            cws[0, 0, 0:HALF] = dot(xin[0:HALF], wall[block]).astype(BF)
            rs_copy(0, 0, 0).start()
            cws[1, 0, HALF:NT] = dot(xin[HALF:NT], wall[block]).astype(BF)
            rs_copy(1, 0, 1).start()
        else:
            for way in range(2):
                block = place_of(t, way)
                gw.use(block)
                part[way] = dot(xin[...], wall[block])
            for turn in range(2):
                for way in range(2):
                    p = turn if way == 0 else 1 - turn
                    rows = slice(p * HALF, (p + 1) * HALF)
                    total = part[way, rows]
                    if t > 1 or turn == 0:
                        rs_copy(way, t - 1, p).wait_recv()
                        total = total + cwr[way, t - 1, rows].astype(F32)
                    cws[way, t, rows] = total.astype(BF)
                    rs_copy(way, t, p).start()
        if t + AHEAD <= 8:
            issue(t + AHEAD)
        if t == 4:
            go.first()
        if t == 6:
            for j in range(NZ):
                go.second(jnp.int32(j))
    gw.use(z)
    part[0] = dot(xin[...], wall[z])
    for p in range(2):
        rows = slice(p * HALF, (p + 1) * HALF)
        for way in range(2):
            rs_copy(way, 7, p).wait_recv()
        total = part[0, rows] + cwr[0, 7, rows].astype(F32) + cwr[1, 7, rows].astype(F32)
        part[1, rows] = total.astype(BF).astype(F32)

    def head_norm(block, gain):
        square = jnp.mean(block * block, axis=-1, keepdims=True)
        return (block * lax.rsqrt(square + 1e-06) * gain).astype(BF)

    ks[y] = head_norm(part[1, :, HD:2 * HD], kg_ref[...])
    vs[y] = jnp.transpose(part[1, :, 2 * HD:3 * HD]).astype(BF)

    def qkv_copy(which, o, me):
        ref = (ks, vs, qs)[which].at[me]
        to = at(x, (y + o) % 4) if which < 2 else at((x + o) % 4, y)
        return pltpu.make_async_remote_copy(
            src_ref=ref, dst_ref=ref,
            send_sem=qkv_s.at[which, o], recv_sem=qkv_r.at[which, o],
            device_id=to, device_id_type=MESH,
        )

    for which in range(2):
        for o in (2, 1, 3):
            qkv_copy(which, o, y).start()
    qs[x] = head_norm(part[1, :, 0:HD], qg_ref[...])
    for o in (2, 1, 3):
        qkv_copy(2, o, x).start()
    for which in range(2):
        for o in (1, 3, 2):
            qkv_copy(which, o, (y + 4 - o) % 4).wait_recv()
    for o in (1, 3, 2):
        qkv_copy(2, o, (x + 4 - o) % 4).wait_recv()

    def nd_copy(which, o):
        src, dst = ((nsend, nrecv), (dsend, drecv))[which]
        return pltpu.make_async_remote_copy(
            src_ref=src.at[o], dst_ref=dst.at[o],
            send_sem=nd_s.at[which, o], recv_sem=nd_r.at[which, o],
            device_id=at((x + o) % 4, y), device_id_type=MESH,
        )

    def attend(queries):
        top = jnp.zeros((HD, NT), F32)
        low = jnp.zeros((1, NT), F32)
        for j in range(4):
            scores = lax.dot_general(
                ks[j], queries, (((1,), (1,)), ((), ())), preferred_element_type=F32
            ) * HD ** (-0.5)
            probs = jnp.exp(scores) * mask[...]
            low = low + jnp.sum(probs, axis=0, keepdims=True)
            top = top + dot(vs[j], probs.astype(BF))
        return top, low

    for o in (2, 1, 3):
        top, low = attend(qs[(x + o) % 4])
        nsend[o] = top.astype(BF)
        dsend[o] = jnp.broadcast_to(low, (8, NT))
        nd_copy(0, o).start()
        nd_copy(1, o).start()
    top, low = attend(qs[x])
    for o in (2, 1, 3):
        nd_copy(0, o).wait_recv()
        nd_copy(1, o).wait_recv()
        top = top + nrecv[o].astype(F32)
        low = low + drecv[o][0:1, :]
    ag[z] = jnp.transpose(top / low).astype(BF)

    def ag_copy(way, t, p, arrival=False):
        back = t + (1 if arrival else 0)
        slot = (z + NZ - back) % NZ if way == 0 else (z + back) % NZ
        ref = ag.at[slot, pl.ds(p * HALF, HALF)]
        return pltpu.make_async_remote_copy(
            src_ref=ref, dst_ref=ref,
            send_sem=ag_s.at[way, t, p], recv_sem=ag_r.at[way, t, p],
            device_id=along_z(1 if way == 0 else NZ - 1), device_id_type=MESH,
        )

    for p in range(2):
        for way in range(2):
            ag_copy(way, 0, p).start()
    for j in range(NZ):
        go.use(jnp.int32(j))
    acc[...] = dot(ag[z], woall[z])
    for t in range(1, 8):
        for turn in range(2):
            for way in range(2):
                p = turn if way == 0 else 1 - turn
                ag_copy(way, t - 1, p, True).wait_recv()
                if t < 7 or turn == 0:
                    ag_copy(way, t, p).start()
        a, b = (z + NZ - t) % NZ, (z + t) % NZ
        acc[...] += dot(ag[a], woall[a]) + dot(ag[b], woall[b])
    ag_copy(0, 7, 0, True).wait_recv()
    ag_copy(1, 7, 1, True).wait_recv()
    a = (z + 8) % NZ
    acc[...] += dot(ag[a], woall[a])

    sibs[...] = acc[pl.ds(pl.multiple_of((1 - core) * HALF, HALF), HALF)].astype(BF)

    sib = pltpu.make_async_remote_copy(
        src_ref=sibs, dst_ref=sibr, send_sem=sib_s.at[1], recv_sem=sib_r.at[1],
        device_id=sibling, device_id_type=MESH,
    )
    sib.start()
    own = acc[pl.ds(pl.multiple_of(core * HALF, HALF), HALF)]
    sib.wait_recv()
    osend[...] = (own + sibr[...].astype(F32)).reshape(NZ, 8, BLK).astype(BF)

    def out_copy(o, arrival=False):
        slot = (z + NZ - o) % NZ if arrival else z
        return pltpu.make_async_remote_copy(
            src_ref=osend.at[(z + o) % NZ], dst_ref=orecv.at[slot],
            send_sem=oa_s.at[o], recv_sem=oa_r.at[o],
            device_id=along_z(o), device_id_type=MESH,
        )

    for o in FAR_FIRST:
        out_copy(o).start()
    orecv[z] = osend[z]

    for o in range(1, NZ):
        x_copy(o).wait_send()
    x_sib(core).wait_send()
    gw.drain()
    go.drain()
    for way in range(2):
        for t in range(8):
            for p in range(2):
                if t > 0 or p == way:
                    rs_copy(way, t, p).wait_send()
                if t < 7 or p == way:
                    ag_copy(way, t, p).wait_send()
    for o in (1, 2, 3):
        for which in range(3):
            qkv_copy(which, o, y if which < 2 else x).wait_send()
        for which in range(2):
            nd_copy(which, o).wait_send()
    sib.wait_send()

    for o in reversed(FAR_FIRST):
        out_copy(o, True).wait_recv()
    for o in range(1, NZ):
        out_copy(o).wait_send()
    for j in range(NZ):
        out_ref[:, j * BLK:(j + 1) * BLK] = orecv[j]


def body(latents, levels, order, level_table, q_gain, k_gain, w_qkv, w_out):
    vmem = pl.BlockSpec(memory_space=pltpu.VMEM)
    smem = pl.BlockSpec(memory_space=pltpu.SMEM)
    hbm = pl.BlockSpec(memory_space=pl.ANY)
    dma = pltpu.SemaphoreType.DMA
    return pl.pallas_call(
        kernel,
        out_shape=jax.ShapeDtypeStruct(latents.shape, BF),
        in_specs=[vmem, smem, smem, vmem, vmem, vmem, hbm, hbm],
        out_specs=vmem,
        scratch_shapes=[
            pltpu.VMEM((16, BLK, BLK), BF),
            pltpu.VMEM((16, HD, BLK), BF),
            pltpu.VMEM((NZ, 8, BLK), BF),
            pltpu.VMEM((2, NZ, 8, BLK), BF),
            pltpu.VMEM((NT, BLK), BF),
            pltpu.VMEM((2, NT, BLK), F32),
            pltpu.VMEM((2, 8, NT, BLK), BF),
            pltpu.VMEM((2, 8, NT, BLK), BF),
            pltpu.VMEM((NT, NT), F32),
            pltpu.VMEM((4, NT, HD), BF),
            pltpu.VMEM((4, NT, HD), BF),
            pltpu.VMEM((4, HD, NT), BF),
            pltpu.VMEM((4, HD, NT), BF),
            pltpu.VMEM((4, HD, NT), BF),
            pltpu.VMEM((4, 8, NT), F32),
            pltpu.VMEM((4, 8, NT), F32),
            pltpu.VMEM((NZ, NT, HD), BF),
            pltpu.VMEM((NT, BLK), F32),
            pltpu.VMEM((HALF, BLK), BF),
            pltpu.VMEM((HALF, BLK), BF),
            pltpu.VMEM((NZ, 8, BLK), BF),
            pltpu.VMEM((NZ, 8, BLK), BF),
            dma((2,)),
            dma((NZ,)), dma((NZ,)),
            dma((2,)), dma((2,)),
            dma((2, 3)), dma((2, 4, 3)), dma((2, 16)),
            dma((2, 3)), dma((2, 4, 3)), dma((2, 16)),
            dma((2, 8, 2)), dma((2, 8, 2)),
            dma((3, 4)), dma((3, 4)),
            dma((2, 4)), dma((2, 4)),
            dma((2, 8, 2)), dma((2, 8, 2)),
            dma((NZ,)), dma((NZ,)),
        ],
        compiler_params=pltpu.CompilerParams(
            collective_id=0, has_side_effects=True, vmem_limit_bytes=40 * 2**20
        ),
        name="spans",
    )(
        latents, levels, order, level_table,
        q_gain.reshape(1, HD), k_gain.reshape(1, HD), w_qkv, w_out,
    )


def solution(mesh):
    placed = (
        P(("span", "seq"), None),
        P("span"),
        P(),
        P(),
        P(),
        P(),
        P("span", "seq"),
        P("seq", "span"),
    )
    return jax.shard_map(
        body, mesh=mesh, in_specs=placed, out_specs=P(("span", "seq"), None), check_vma=False
    )
```

time: 484 us -> 149 us (0.31)
  waiting for transfers between devices: 448 us -> 0 us
  Pallas kernels: 0 us -> 143 us
  between operations: 14.2 us -> 0.69 us
  matrix products: 12.9 us -> 0 us
  other arithmetic: 6.99 us -> 0 us
    all_gather x5 -> x0, waiting for transfers between devices: 337 us -> none  [the longest x1 69.8 us: body(): val_piece = lax.all_gather(vals, 'span', axis=0, tiled=True)]
    pallas_call x0 -> x1, Pallas kernels: none -> 143 us  [body(): pl.pallas_call(kernel, out_shape=jax.ShapeDtypeStruct(latents.shape, BF),...]
    reduce_scatter x1 -> x0, waiting for transfers between devices: 109 us -> none  [body(): lax.psum_scatter(terms.astype(jnp.bfloat16), 'seq', scatter_dimension=0,...]
    dot_general x3 -> x0, matrix products: 12.9 us -> none  [the longest x1 6.08 us: body(): jnp.dot(attn, lax.all_gather(w_out, 'span', axis=1, tiled=True), preferre...]
    unnamed x8 -> x15, local copies, waits for them, and re-layouts: 0.29 us -> 5.18 us
  transfers between devices with their start and end apart: 6 -> 0, of which waited for: 6 -> 0; matrix products, arithmetic and copies ran while one was open for 2% -> 0% of each run, Pallas kernels for 0% -> 0%
where the time goes in v1:
time: 149 us
  Pallas kernels  143 us (96%)
  local copies, waits for them, and re-layouts  5.18 us (3%)
    pallas_call x1, Pallas kernels, body(): pl.pallas_call(kernel, out_shape=jax.ShapeDtypeStruct(latents.shape, BF),...  143 us
    unnamed x15, local copies, waits for them, and re-layouts  5.18 us

profile of v1, /device:TPU:1, one launch (start us, length us, event | category | flops | bytes accessed | tf_op | source)
XLA Modules:
  0.0 148.8 jit_solution(6177415032165558802)
XLA Ops:
  0.7 0.0 copy-start.4
  0.7 0.0 copy-start.5
  0.7 0.0 copy-start.6
  0.7 0.6 copy-done.4
  1.3 0.0 copy-done.5
  1.3 0.0 copy-done.6
  1.3 0.0 copy-start
  1.3 1.1 copy-done
  2.5 0.0 copy-start.1
  2.5 1.0 copy-done.1
  3.4 0.0 copy-start.2
  3.4 0.9 copy-done.2
  4.3 0.0 copy-start.3
  4.3 0.9 copy-done.3
  5.2 142.9 %spans.1 = bf16[8,6144]{1,0:T(8,128)(2,1)S(1)} custom-call(bf16[8,6144]{1,0:T(8,128)(2,1)S(1)} %copy-done.2, s32[1]{0:T(128)S(6)} %copy.10.lev_ref, s32[16]{0:T(128)S(1)} %copy-done.4, f32[16,12288]{1,0:T(8,128)S(1)} %copy-done, f32[1,128]{1,0:T(1,128)S(1)} %bitcast.2, f32[1,128]{1,0:T(1,128)S(1)} %bitcast.3, bf16[384,384]{1,0:T(8,128)(2,1)S(1)} %copy-done.1, ...), custom_call_target="tpu_custom_call" | custom-call | tf_op jit(solution)/shard_map/spans/pallas_call | solution.py:396
  148.1 0.6 copy.11
Async XLA Ops:
  0.7 0.7 copy-start.4
  0.7 0.7 copy-start.5
  0.7 0.7 copy-start.6
  1.3 1.1 copy-start
  2.5 1.0 copy-start.1
  3.4 0.9 copy-start.2
  4.3 0.9 copy-start.3

commit v2 on v1

--- a/solution.py
+++ b/solution.py
@@ -14,7 +14,7 @@
 NT = 256
 HALF = 128
 FAR_FIRST = (8, 7, 9, 6, 10, 5, 11, 4, 12, 3, 13, 2, 14, 1, 15)
-AHEAD = 3
+FIRST = 4
 
 
 def dot(a, b):
@@ -25,7 +25,11 @@
     def __init__(self, buf, rows, x, y, at, s1, s2, rs):
         self.buf, self.rows, self.x, self.y, self.at = buf, rows, x, y, at
         self.s1, self.s2, self.rs = s1, s2, rs
-        self.mine = y * 4 + x
+        self.mine = ((x + 4 - y) % 4) * 4 + y
+
+    @staticmethod
+    def place(block):
+        return block % 4, (block + block // 4) % 4
 
     def part(self, block, half):
         return self.buf.at[block, pl.ds(half * self.rows, self.rows)]
@@ -58,7 +62,7 @@
         self.copy(block, half, 1, 0).wait_recv()
 
     def second(self, block):
-        by, bx = block // 4, block % 4
+        by, bx = self.place(block)
         for half in range(2):
             same = (by == self.y) if half == 0 else (bx == self.x)
             slot = bx if half == 0 else by
@@ -73,7 +77,7 @@
                     self.copy(block, half, 2, i, slot).start()
 
     def use(self, block):
-        by, bx = block // 4, block % 4
+        by, bx = self.place(block)
 
         @pl.when(by != self.y)
         def _():
@@ -92,8 +96,8 @@
 
 
 def kernel(
-    lat_ref, lev_ref, ord_ref, tab_ref, qg_ref, kg_ref, w_ref, wo_ref, out_ref,
-    wall, woall, xsend, xr, xin, part, cws, cwr, mask,
+    lat_hbm, lev_ref, ord_ref, tab_hbm, qg_hbm, kg_hbm, w_ref, wo_ref, out_ref,
+    lat_ref, tab_ref, qg_ref, kg_ref, wall, woall, xsend, xr, xin, part, cws, cwr, mask,
     qs, ks, vs, nsend, nrecv, dsend, drecv, ag, acc, sibs, sibr, osend, orecv,
     load_sem, xa_s, xa_r, sib_s, sib_r, w1, w2, wr, o1, o2, orr,
     rs_s, rs_r, qkv_s, qkv_r, nd_s, nd_r, ag_s, ag_r, oa_s, oa_r,
@@ -113,10 +117,17 @@
 
     sibling = (z, chip * 2 + 1 - core)
 
-    load_w = pltpu.make_async_copy(w_ref, wall.at[chip], load_sem.at[0])
-    load_o = pltpu.make_async_copy(wo_ref, woall.at[chip], load_sem.at[1])
-    load_w.start()
-    load_o.start()
+    gw = PlaneGather(wall, BLK // 2, x, y, at, w1, w2, wr)
+    go = PlaneGather(woall, HD // 2, x, y, at, o1, o2, orr)
+    loads = [
+        pltpu.make_async_copy(src, dst, load_sem.at[i])
+        for i, (src, dst) in enumerate((
+            (lat_hbm, lat_ref), (tab_hbm, tab_ref), (w_ref, wall.at[gw.mine]),
+            (wo_ref, woall.at[go.mine]), (qg_hbm, qg_ref), (kg_hbm, kg_ref),
+        ))
+    ]
+    for load in loads:
+        load.start()
 
     barrier = pltpu.get_barrier_semaphore()
     for o in FAR_FIRST:
@@ -126,6 +137,8 @@
         pl.semaphore_signal(barrier, inc=1, device_id=at(x, (y + o) % 4), device_id_type=MESH)
     pl.semaphore_signal(barrier, inc=1, device_id=sibling, device_id_type=MESH)
 
+    for load in loads:
+        load.wait()
     width = lat_ref.shape[1]
     level = lev_ref[0]
     row = tab_ref[pl.ds(level, 1), :]
@@ -138,9 +151,6 @@
         xsend[j] = modulated[:, j * BLK:(j + 1) * BLK]
     xr[core, z] = xsend[z]
 
-    gw = PlaneGather(wall, BLK // 2, x, y, at, w1, w2, wr)
-    go = PlaneGather(woall, HD // 2, x, y, at, o1, o2, orr)
-
     def x_copy(o):
         return pltpu.make_async_remote_copy(
             src_ref=xsend.at[(z + o) % NZ], dst_ref=xr.at[core, z],
@@ -155,8 +165,6 @@
             device_id=along_z(o), device_id_type=MESH,
         )
 
-    load_w.wait()
-    load_o.wait()
     pl.semaphore_wait(barrier, 22)
     for o in FAR_FIRST:
         x_copy(o).start()
@@ -188,13 +196,12 @@
     def place_of(t, way):
         return (z + 8 - t) % NZ if way == 0 else (z + 8 + t) % NZ
 
-    def issue(t):
-        gw.second(place_of(t, 0))
-        if 0 < t < 8:
-            gw.second(place_of(t, 1))
-
-    for t in range(AHEAD):
-        issue(t)
+    order_of_use = [place_of(0, 0)]
+    for t in range(1, 8):
+        order_of_use += [place_of(t, 0), place_of(t, 1)]
+    order_of_use.append(z)
+    for block in order_of_use[:FIRST]:
+        gw.second(block)
 
     x_sib(1 - core).wait_recv()
     xin[...] = xr[...].astype(F32).reshape(NT, BLK).astype(BF)
@@ -230,12 +237,12 @@
                         total = total + cwr[way, t - 1, rows].astype(F32)
                     cws[way, t, rows] = total.astype(BF)
                     rs_copy(way, t, p).start()
-        if t + AHEAD <= 8:
-            issue(t + AHEAD)
-        if t == 4:
+        for block in order_of_use[FIRST + 2 * t:FIRST + 2 * t + 2]:
+            gw.second(block)
+        if t == 3:
             go.first()
-        if t == 6:
-            for j in range(NZ):
+        if t > 3:
+            for j in range(4 * (t - 4), 4 * (t - 3)):
                 go.second(jnp.int32(j))
     gw.use(z)
     part[0] = dot(xin[...], wall[z])
@@ -323,7 +330,6 @@
             ag_copy(way, 0, p).start()
     for j in range(NZ):
         go.use(jnp.int32(j))
-    acc[...] = dot(ag[z], woall[z])
     for t in range(1, 8):
         for turn in range(2):
             for way in range(2):
@@ -331,12 +337,10 @@
                 ag_copy(way, t - 1, p, True).wait_recv()
                 if t < 7 or turn == 0:
                     ag_copy(way, t, p).start()
-        a, b = (z + NZ - t) % NZ, (z + t) % NZ
-        acc[...] += dot(ag[a], woall[a]) + dot(ag[b], woall[b])
     ag_copy(0, 7, 0, True).wait_recv()
     ag_copy(1, 7, 1, True).wait_recv()
-    a = (z + 8) % NZ
-    acc[...] += dot(ag[a], woall[a])
+    gathered = jnp.concatenate([ag[j] for j in range(NZ)], axis=1)
+    acc[...] = dot(gathered, woall[...].reshape(NZ * HD, BLK))
 
     sibs[...] = acc[pl.ds(pl.multiple_of((1 - core) * HALF, HALF), HALF)].astype(BF)
 
@@ -396,9 +400,13 @@
     return pl.pallas_call(
         kernel,
         out_shape=jax.ShapeDtypeStruct(latents.shape, BF),
-        in_specs=[vmem, smem, smem, vmem, vmem, vmem, hbm, hbm],
+        in_specs=[hbm, smem, smem, hbm, hbm, hbm, hbm, hbm],
         out_specs=vmem,
         scratch_shapes=[
+            pltpu.VMEM(latents.shape, BF),
+            pltpu.VMEM(level_table.shape, F32),
+            pltpu.VMEM((1, HD), F32),
+            pltpu.VMEM((1, HD), F32),
             pltpu.VMEM((16, BLK, BLK), BF),
             pltpu.VMEM((16, HD, BLK), BF),
             pltpu.VMEM((NZ, 8, BLK), BF),
@@ -421,7 +429,7 @@
             pltpu.VMEM((HALF, BLK), BF),
             pltpu.VMEM((NZ, 8, BLK), BF),
             pltpu.VMEM((NZ, 8, BLK), BF),
-            dma((2,)),
+            dma((6,)),
             dma((NZ,)), dma((NZ,)),
             dma((2,)), dma((2,)),
             dma((2, 3)), dma((2, 4, 3)), dma((2, 16)),
@@ -433,7 +441,7 @@
             dma((NZ,)), dma((NZ,)),
         ],
         compiler_params=pltpu.CompilerParams(
-            collective_id=0, has_side_effects=True, vmem_limit_bytes=40 * 2**20
+            collective_id=0, has_side_effects=True, vmem_limit_bytes=60 * 2**20
         ),
         name="spans",
     )(

time: 149 us -> 131 us (0.88)
  Pallas kernels: 143 us -> 128 us
  local copies, waits for them, and re-layouts: 5.18 us -> 1.54 us
    pallas_call x1, Pallas kernels: 143 us -> 128 us  [body(): pl.pallas_call(kernel, out_shape=jax.ShapeDtypeStruct(latents.shape, BF),...]
    unnamed x15 -> x1, local copies, waits for them, and re-layouts: 5.18 us -> 1.54 us
where the time goes in v2:
time: 131 us; the launch traced here: 130 us
  Pallas kernels  128 us (98%)
  local copies, waits for them, and re-layouts  1.54 us (1%)
    pallas_call x1, Pallas kernels, body(): pl.pallas_call(kernel, out_shape=jax.ShapeDtypeStruct(latents.shape, BF),...  128 us

profile of v2, /device:TPU:1, one launch (start us, length us, event | category | flops | bytes accessed | tf_op | source)
XLA Modules:
  0.0 130.3 jit_solution(9169448280589514660)
XLA Ops:
  0.7 128.1 %spans.1 = bf16[8,6144]{1,0:T(8,128)(2,1)} custom-call(bf16[8,6144]{1,0:T(8,128)(2,1)} %lat_hbm.1, s32[1]{0:T(128)S(6)} %copy.10.lev_ref, s32[16]{0:T(128)} %ord_ref.1, f32[16,12288]{1,0:T(8,128)} %tab_hbm.1, f32[1,128]{1,0:T(1,128)} %bitcast.2, f32[1,128]{1,0:T(1,128)} %bitcast.3, bf16[384,384]{1,0:T(8,128)(2,1)} %w_ref.1, bf16[128,384]{1,0:T(8,128)(2,1)} %wo_ref.1), custom_call_target="tpu_custom_call" | custom-call | tf_op jit(solution)/shard_map/spans/pallas_call | solution.py:400
  128.8 1.5 %copy.11 = bf16[8,6144]{1,0:T(8,128)(2,1)} copy(bf16[8,6144]{1,0:T(8,128)(2,1)} %spans.1) | data formatting | bytes 196608

commit v3 on v2

--- a/solution.py
+++ b/solution.py
@@ -15,6 +15,9 @@
 HALF = 128
 FAR_FIRST = (8, 7, 9, 6, 10, 5, 11, 4, 12, 3, 13, 2, 14, 1, 15)
 FIRST = 4
+WO_AT = {0: 3, 3: 4, 6: 5}
+PIECES = 2
+WIDE = 8 * BLK // PIECES
 
 
 def dot(a, b):
@@ -97,10 +100,10 @@
 
 def kernel(
     lat_hbm, lev_ref, ord_ref, tab_hbm, qg_hbm, kg_hbm, w_ref, wo_ref, out_ref,
-    lat_ref, tab_ref, qg_ref, kg_ref, wall, woall, xsend, xr, xin, part, cws, cwr, mask,
-    qs, ks, vs, nsend, nrecv, dsend, drecv, ag, acc, sibs, sibr, osend, orecv,
-    load_sem, xa_s, xa_r, sib_s, sib_r, w1, w2, wr, o1, o2, orr,
-    rs_s, rs_r, qkv_s, qkv_r, nd_s, nd_r, ag_s, ag_r, oa_s, oa_r,
+    lat_ref, tab_ref, qg_ref, kg_ref, wall, xsend, xr, xin, part, cws, cwr, mask,
+    qs, ks, vs, nsend, nrecv, dsend, drecv, wog, asend, brecv, ts, tr, us, ur,
+    load_sem, xa_s, xa_r, sib_s, sib_r, w1, w2, wr, wo_s, wo_r, ws_s, ws_r,
+    rs_s, rs_r, qkv_s, qkv_r, nd_s, nd_r, aa_s, aa_r, t_s, t_r, u_s, u_r,
 ):
     z = lax.axis_index("span")
     s = lax.axis_index("seq")
@@ -118,12 +121,11 @@
     sibling = (z, chip * 2 + 1 - core)
 
     gw = PlaneGather(wall, BLK // 2, x, y, at, w1, w2, wr)
-    go = PlaneGather(woall, HD // 2, x, y, at, o1, o2, orr)
     loads = [
         pltpu.make_async_copy(src, dst, load_sem.at[i])
         for i, (src, dst) in enumerate((
             (lat_hbm, lat_ref), (tab_hbm, tab_ref), (w_ref, wall.at[gw.mine]),
-            (wo_ref, woall.at[go.mine]), (qg_hbm, qg_ref), (kg_hbm, kg_ref),
+            (wo_ref, wog.at[core, z]), (qg_hbm, qg_ref), (kg_hbm, kg_ref),
         ))
     ]
     for load in loads:
@@ -166,9 +168,43 @@
         )
 
     pl.semaphore_wait(barrier, 22)
+    gw.first()
     for o in FAR_FIRST:
         x_copy(o).start()
-    gw.first()
+
+    def wo_copy(way, t, arrival=False):
+        back = t + (1 if arrival else 0)
+        slot = (z + NZ - back) % NZ if way == 0 else (z + back) % NZ
+        ref = wog.at[core, slot]
+        if t == 7:
+            ref = wog.at[core, slot, pl.ds(way * (HD // 2), HD // 2)]
+        return pltpu.make_async_remote_copy(
+            src_ref=ref, dst_ref=ref,
+            send_sem=wo_s.at[way, t], recv_sem=wo_r.at[way, t],
+            device_id=along_z(1 if way == 0 else NZ - 1), device_id_type=MESH,
+        )
+
+    def wo_sib(side, o):
+        ref = wog.at[side, (z + o) % NZ]
+        return pltpu.make_async_remote_copy(
+            src_ref=ref, dst_ref=ref, send_sem=ws_s.at[o], recv_sem=ws_r.at[o],
+            device_id=sibling, device_id_type=MESH,
+        )
+
+    def wo_step(t):
+        if t > 0:
+            for way in range(2):
+                wo_copy(way, t - 1, True).wait_recv()
+        if t < 8:
+            for way in range(2):
+                wo_copy(way, t).start()
+        if t == 0 or t == 8:
+            wo_sib(core, t).start()
+        else:
+            wo_sib(core, t).start()
+            wo_sib(core, NZ - t).start()
+
+    wo_step(0)
 
     key_span = (lax.broadcasted_iota(jnp.int32, (NT, HD), 0) % HALF) // 8
     query_span = (lax.broadcasted_iota(jnp.int32, (8, NT), 1) % HALF) // 8
@@ -203,8 +239,11 @@
     for block in order_of_use[:FIRST]:
         gw.second(block)
 
+    wo_step(1)
     x_sib(1 - core).wait_recv()
     xin[...] = xr[...].astype(F32).reshape(NT, BLK).astype(BF)
+
+    wo_step(2)
 
     def rs_copy(way, t, p):
         rows = pl.ds(p * HALF, HALF)
@@ -239,11 +278,8 @@
                     rs_copy(way, t, p).start()
         for block in order_of_use[FIRST + 2 * t:FIRST + 2 * t + 2]:
             gw.second(block)
-        if t == 3:
-            go.first()
-        if t > 3:
-            for j in range(4 * (t - 4), 4 * (t - 3)):
-                go.second(jnp.int32(j))
+        if t in WO_AT:
+            wo_step(WO_AT[t])
     gw.use(z)
     part[0] = dot(xin[...], wall[z])
     for p in range(2):
@@ -275,6 +311,7 @@
     qs[x] = head_norm(part[1, :, 0:HD], qg_ref[...])
     for o in (2, 1, 3):
         qkv_copy(2, o, x).start()
+    wo_step(6)
     for which in range(2):
         for o in (1, 3, 2):
             qkv_copy(which, o, (y + 4 - o) % 4).wait_recv()
@@ -307,89 +344,136 @@
         dsend[o] = jnp.broadcast_to(low, (8, NT))
         nd_copy(0, o).start()
         nd_copy(1, o).start()
+        if o == 1:
+            wo_step(7)
     top, low = attend(qs[x])
+    wo_step(8)
     for o in (2, 1, 3):
         nd_copy(0, o).wait_recv()
         nd_copy(1, o).wait_recv()
         top = top + nrecv[o].astype(F32)
         low = low + drecv[o][0:1, :]
-    ag[z] = jnp.transpose(top / low).astype(BF)
-
-    def ag_copy(way, t, p, arrival=False):
-        back = t + (1 if arrival else 0)
-        slot = (z + NZ - back) % NZ if way == 0 else (z + back) % NZ
-        ref = ag.at[slot, pl.ds(p * HALF, HALF)]
-        return pltpu.make_async_remote_copy(
-            src_ref=ref, dst_ref=ref,
-            send_sem=ag_s.at[way, t, p], recv_sem=ag_r.at[way, t, p],
-            device_id=along_z(1 if way == 0 else NZ - 1), device_id_type=MESH,
-        )
-
-    for p in range(2):
-        for way in range(2):
-            ag_copy(way, 0, p).start()
-    for j in range(NZ):
-        go.use(jnp.int32(j))
-    for t in range(1, 8):
-        for turn in range(2):
-            for way in range(2):
-                p = turn if way == 0 else 1 - turn
-                ag_copy(way, t - 1, p, True).wait_recv()
-                if t < 7 or turn == 0:
-                    ag_copy(way, t, p).start()
-    ag_copy(0, 7, 0, True).wait_recv()
-    ag_copy(1, 7, 1, True).wait_recv()
-    gathered = jnp.concatenate([ag[j] for j in range(NZ)], axis=1)
-    acc[...] = dot(gathered, woall[...].reshape(NZ * HD, BLK))
-
-    sibs[...] = acc[pl.ds(pl.multiple_of((1 - core) * HALF, HALF), HALF)].astype(BF)
-
-    sib = pltpu.make_async_remote_copy(
-        src_ref=sibs, dst_ref=sibr, send_sem=sib_s.at[1], recv_sem=sib_r.at[1],
-        device_id=sibling, device_id_type=MESH,
-    )
-    sib.start()
-    own = acc[pl.ds(pl.multiple_of(core * HALF, HALF), HALF)]
-    sib.wait_recv()
-    osend[...] = (own + sibr[...].astype(F32)).reshape(NZ, 8, BLK).astype(BF)
-
-    def out_copy(o, arrival=False):
-        slot = (z + NZ - o) % NZ if arrival else z
-        return pltpu.make_async_remote_copy(
-            src_ref=osend.at[(z + o) % NZ], dst_ref=orecv.at[slot],
-            send_sem=oa_s.at[o], recv_sem=oa_r.at[o],
-            device_id=along_z(o), device_id_type=MESH,
+    asend[...] = jnp.transpose(top / low).reshape(2, NZ, 8, HD).astype(BF)
+
+    home_y, home_x = gw.place(z)
+    home = home_y * 4 + home_x
+    slot = x * 4 + y
+
+    def aa_copy(side, o):
+        way = jnp.where(side == core, 0, 1)
+        return pltpu.make_async_remote_copy(
+            src_ref=asend.at[side, (z + o) % NZ], dst_ref=brecv.at[slot, core],
+            send_sem=aa_s.at[way, o], recv_sem=aa_r.at[core, slot],
+            device_id=((z + o) % NZ, home * 2 + side), device_id_type=MESH,
+        )
+
+    def aa_arrival(side, i):
+        return pltpu.make_async_remote_copy(
+            src_ref=asend.at[core, z], dst_ref=brecv.at[i, side],
+            send_sem=aa_s.at[0, 0], recv_sem=aa_r.at[side, i],
+            device_id=(gw.mine, ((i % 4) * 4 + i // 4) * 2 + side), device_id_type=MESH,
         )
 
     for o in FAR_FIRST:
-        out_copy(o).start()
-    orecv[z] = osend[z]
+        aa_copy(core, o).start()
+        aa_copy(1 - core, o).start()
+    aa_copy(1 - core, 0).start()
+
+    @pl.when(home != chip)
+    def _():
+        aa_copy(core, 0).start()
+
+    @pl.when(home == chip)
+    def _():
+        brecv[slot, core] = asend[core, z]
+
+    for o in range(NZ):
+        wo_sib(1 - core, o).wait_recv()
+    for i in range(NZ):
+        aa_arrival(1 - core, i).wait_recv()
+
+        @pl.when((home != chip) | (slot != i))
+        def _(i=i):
+            aa_arrival(core, i).wait_recv()
+
+    rows = [brecv[:, k].astype(F32).reshape(HALF, HD).astype(BF) for k in range(2)]
+    rows = jnp.concatenate(rows, axis=1)
+
+    def sum_copy(phase, half, p, o):
+        along_x = (half == 0) == (phase == 0)
+        to = at((x + o) % 4, y) if along_x else at(x, (y + o) % 4)
+        slot = ((x if along_x else y) + o) % 4
+        src, dst, ss, sr = ((ts, tr, t_s, t_r), (us, ur, u_s, u_r))[phase]
+        return pltpu.make_async_remote_copy(
+            src_ref=src.at[half, p, slot], dst_ref=dst.at[half, p, o],
+            send_sem=ss.at[half, p, o], recv_sem=sr.at[half, p, o],
+            device_id=to, device_id_type=MESH,
+        )
+
+    per = WIDE // BLK
+    for p in range(PIECES):
+        for half in range(2):
+            for i in range(per):
+                j = half * 8 + p * per + i
+                cols = slice(i * BLK, (i + 1) * BLK)
+                term = dot(rows, jnp.concatenate([wog[0, j], wog[1, j]], axis=0))
+                term = term.reshape(4, 4, 8, BLK)
+                for q in range(4):
+                    mine = term[q] if half == 0 else term[:, q]
+                    ts[half, p, q, :, cols] = mine.reshape(32, BLK).astype(BF)
+            for o in (2, 1, 3):
+                sum_copy(0, half, p, o).start()
+    for p in range(PIECES):
+        for half in range(2):
+            total = ts[half, p, x if half == 0 else y].astype(F32)
+            for o in (1, 3, 2):
+                sum_copy(0, half, p, o).wait_recv()
+                total = total + tr[half, p, o].astype(F32)
+            us[half, p] = total.reshape(4, 8, WIDE).astype(BF)
+            for o in (2, 1, 3):
+                sum_copy(1, half, p, o).start()
 
     for o in range(1, NZ):
         x_copy(o).wait_send()
     x_sib(core).wait_send()
     gw.drain()
-    go.drain()
     for way in range(2):
         for t in range(8):
+            wo_copy(way, t).wait_send()
             for p in range(2):
                 if t > 0 or p == way:
                     rs_copy(way, t, p).wait_send()
-                if t < 7 or p == way:
-                    ag_copy(way, t, p).wait_send()
+    for o in range(NZ):
+        wo_sib(core, o).wait_send()
+        aa_copy(1 - core, o).wait_send()
+        if o > 0:
+            aa_copy(core, o).wait_send()
+
+    @pl.when(home != chip)
+    def _():
+        aa_copy(core, 0).wait_send()
+
     for o in (1, 2, 3):
         for which in range(3):
             qkv_copy(which, o, y if which < 2 else x).wait_send()
         for which in range(2):
             nd_copy(which, o).wait_send()
-    sib.wait_send()
-
-    for o in reversed(FAR_FIRST):
-        out_copy(o, True).wait_recv()
-    for o in range(1, NZ):
-        out_copy(o).wait_send()
-    for j in range(NZ):
-        out_ref[:, j * BLK:(j + 1) * BLK] = orecv[j]
+        for half in range(2):
+            for p in range(PIECES):
+                sum_copy(0, half, p, o).wait_send()
+
+    for p in range(PIECES):
+        for half in range(2):
+            total = us[half, p, y if half == 0 else x].astype(F32)
+            for o in (1, 3, 2):
+                sum_copy(1, half, p, o).wait_recv()
+                total = total + ur[half, p, o].astype(F32)
+            first = half * 8 * BLK + p * WIDE
+            out_ref[:, first:first + WIDE] = total.astype(BF)
+    for o in (1, 2, 3):
+        for half in range(2):
+            for p in range(PIECES):
+                sum_copy(1, half, p, o).wait_send()
 
 
 def body(latents, levels, order, level_table, q_gain, k_gain, w_qkv, w_out):
@@ -408,7 +492,6 @@
             pltpu.VMEM((1, HD), F32),
             pltpu.VMEM((1, HD), F32),
             pltpu.VMEM((16, BLK, BLK), BF),
-            pltpu.VMEM((16, HD, BLK), BF),
             pltpu.VMEM((NZ, 8, BLK), BF),
             pltpu.VMEM((2, NZ, 8, BLK), BF),
             pltpu.VMEM((NT, BLK), BF),
@@ -423,22 +506,25 @@
             pltpu.VMEM((4, HD, NT), BF),
             pltpu.VMEM((4, 8, NT), F32),
             pltpu.VMEM((4, 8, NT), F32),
-            pltpu.VMEM((NZ, NT, HD), BF),
-            pltpu.VMEM((NT, BLK), F32),
-            pltpu.VMEM((HALF, BLK), BF),
-            pltpu.VMEM((HALF, BLK), BF),
-            pltpu.VMEM((NZ, 8, BLK), BF),
-            pltpu.VMEM((NZ, 8, BLK), BF),
+            pltpu.VMEM((2, NZ, HD, BLK), BF),
+            pltpu.VMEM((2, NZ, 8, HD), BF),
+            pltpu.VMEM((NZ, 2, 8, HD), BF),
+            pltpu.VMEM((2, PIECES, 4, 32, WIDE), BF),
+            pltpu.VMEM((2, PIECES, 4, 32, WIDE), BF),
+            pltpu.VMEM((2, PIECES, 4, 8, WIDE), BF),
+            pltpu.VMEM((2, PIECES, 4, 8, WIDE), BF),
             dma((6,)),
             dma((NZ,)), dma((NZ,)),
-            dma((2,)), dma((2,)),
+            dma((1,)), dma((1,)),
             dma((2, 3)), dma((2, 4, 3)), dma((2, 16)),
-            dma((2, 3)), dma((2, 4, 3)), dma((2, 16)),
+            dma((2, 8)), dma((2, 8)),
+            dma((NZ,)), dma((NZ,)),
             dma((2, 8, 2)), dma((2, 8, 2)),
             dma((3, 4)), dma((3, 4)),
             dma((2, 4)), dma((2, 4)),
-            dma((2, 8, 2)), dma((2, 8, 2)),
-            dma((NZ,)), dma((NZ,)),
+            dma((2, NZ)), dma((2, NZ)),
+            dma((2, PIECES, 4)), dma((2, PIECES, 4)),
+            dma((2, PIECES, 4)), dma((2, PIECES, 4)),
         ],
         compiler_params=pltpu.CompilerParams(
             collective_id=0, has_side_effects=True, vmem_limit_bytes=60 * 2**20

time: 131 us -> 117 us (0.89)
  Pallas kernels: 128 us -> 114 us
    pallas_call x1, Pallas kernels: 128 us -> 114 us  [body(): pl.pallas_call(kernel, out_shape=jax.ShapeDtypeStruct(latents.shape, BF),...]
where the time goes in v3:
time: 117 us; the launch traced here: 116 us
  Pallas kernels  114 us (97%)
  local copies, waits for them, and re-layouts  1.54 us (1%)
    pallas_call x1, Pallas kernels, body(): pl.pallas_call(kernel, out_shape=jax.ShapeDtypeStruct(latents.shape, BF),...  114 us

profile of v3, /device:TPU:1, one launch (start us, length us, event | category | flops | bytes accessed | tf_op | source)
XLA Modules:
  0.0 115.9 jit_solution(16847049977104076122)
XLA Ops:
  0.7 113.7 %spans.1 = bf16[8,6144]{1,0:T(8,128)(2,1)} custom-call(bf16[8,6144]{1,0:T(8,128)(2,1)} %lat_hbm.1, s32[1]{0:T(128)S(6)} %copy.10.lev_ref, s32[16]{0:T(128)} %ord_ref.1, f32[16,12288]{1,0:T(8,128)} %tab_hbm.1, f32[1,128]{1,0:T(1,128)} %bitcast.2, f32[1,128]{1,0:T(1,128)} %bitcast.3, bf16[384,384]{1,0:T(8,128)(2,1)} %w_ref.1, bf16[128,384]{1,0:T(8,128)(2,1)} %wo_ref.1), custom_call_target="tpu_custom_call" | custom-call | tf_op jit(solution)/shard_map/spans/pallas_call | solution.py:484
  114.4 1.5 %copy.11 = bf16[8,6144]{1,0:T(8,128)(2,1)} copy(bf16[8,6144]{1,0:T(8,128)(2,1)} %spans.1) | data formatting | bytes 196608

commit v4 on v3

v4 whole, which is shorter than its diff:
```python
import jax
import jax.numpy as jnp
from jax import lax
from jax.experimental import pallas as pl
from jax.experimental.pallas import tpu as pltpu
from jax.sharding import PartitionSpec as P

HD = 128
NZ = 16
BF = jnp.bfloat16
F32 = jnp.float32
MESH = pl.DeviceIdType.MESH
BLK = 384
NT = 256
HALF = 128
FAR_FIRST = (8, 7, 9, 6, 10, 5, 11, 4, 12, 3, 13, 2, 14, 1, 15)
FIRST = 6
PARTS = 1
WO_AT = {0: 3, 3: 4, 6: 5}
PIECES = 2
WIDE = 8 * BLK // PIECES


def dot(a, b):
    return jnp.dot(a, b, preferred_element_type=F32)


def take(ref, sem):
    pltpu.make_async_copy(ref, ref, sem).wait()


class PlaneGather:
    def __init__(self, buf, rows, x, y, at, s1, rs):
        self.buf, self.rows, self.x, self.y, self.at = buf, rows, x, y, at
        self.s1, self.rs = s1, rs
        self.mine = ((x + 4 - y) % 4) * 4 + y

    @staticmethod
    def place(block):
        return block % 4, (block + block // 4) % 4

    def part(self, block, half, part):
        rows = self.rows // PARTS
        return self.buf.at[block, pl.ds(half * self.rows + part * rows, rows)]

    def target(self, half, phase, o):
        along_x = (half == 0) == (phase == 1)
        if along_x:
            return self.at((self.x + o) % 4, self.y)
        return self.at(self.x, (self.y + o) % 4)

    def copy(self, block, half, part, phase, i):
        o = (1, 3, 2)[i]
        sem = self.s1.at[phase - 1, half, i]
        ref = self.part(block, half, part)
        return pltpu.make_async_remote_copy(
            src_ref=ref,
            dst_ref=ref,
            send_sem=sem,
            recv_sem=self.rs.at[half, part, block],
            device_id=self.target(half, phase, o),
            device_id_type=MESH,
        )

    def first(self):
        for part in range(PARTS):
            for i in range(3):
                for half in range(2):
                    self.copy(self.mine, half, part, 1, i).start()

    def wait_block(self, block, half, part):
        self.copy(block, half, part, 1, 0).wait_recv()

    def second(self, block, part):
        by, bx = self.place(block)
        for half in range(2):
            same = (by == self.y) if half == 0 else (bx == self.x)

            @pl.when(same)
            def _(half=half):
                @pl.when(block != self.mine)
                def _():
                    self.wait_block(block, half, part)

                for i in range(3):
                    self.copy(block, half, part, 2, i).start()

    def use(self, block):
        by, bx = self.place(block)

        @pl.when(by != self.y)
        def _():
            for part in range(PARTS):
                self.wait_block(block, 0, part)

        @pl.when(bx != self.x)
        def _():
            for part in range(PARTS):
                self.wait_block(block, 1, part)

    def drain(self):
        for half in range(2):
            for i in range(3):
                self.copy(self.mine, half, 0, 1, i).wait_send()
                take(self.buf.at[pl.ds(0, 2)], self.s1.at[1, half, i])


def kernel(
    lat_hbm, lev_ref, ord_ref, tab_hbm, qg_hbm, kg_hbm, w_ref, wo_ref, out_ref,
    lat_ref, tab_ref, qg_ref, kg_ref, wall, xsend, xr, xin, part, cws, cwr, mask,
    qs, ks, vs, nsend, nrecv, dsend, drecv, tops, lows, wog, asend, brecv, ts, tr, us, ur,
    load_sem, xa_s, xa_r, sib_s, sib_r, w1, wr, wo_s, wo_r, ws_s, ws_r,
    rs_s, rs_r, qkv_s, qkv_r, nd_s, nd_r, aa_s, aa_r, t_s, t_r, u_s, u_r,
):
    z = lax.axis_index("span")
    s = lax.axis_index("seq")
    core = s % 2
    chip = s // 2
    x = chip % 4
    y = chip // 4

    def at(px, py):
        return (z, (py * 4 + px) * 2 + core)

    def along_z(o):
        return ((z + o) % NZ, s)

    sibling = (z, chip * 2 + 1 - core)

    gw = PlaneGather(wall, BLK // 2, x, y, at, w1, wr)
    loads = [
        pltpu.make_async_copy(src, dst, load_sem.at[i])
        for i, (src, dst) in enumerate((
            (lat_hbm, lat_ref), (tab_hbm, tab_ref), (w_ref, wall.at[gw.mine]),
            (wo_ref, wog.at[core, z]), (qg_hbm, qg_ref), (kg_hbm, kg_ref),
        ))
    ]
    for load in loads:
        load.start()

    barrier = pltpu.get_barrier_semaphore()
    for o in FAR_FIRST:
        pl.semaphore_signal(barrier, inc=1, device_id=along_z(o), device_id_type=MESH)
    for o in (2, 1, 3):
        pl.semaphore_signal(barrier, inc=1, device_id=at((x + o) % 4, y), device_id_type=MESH)
        pl.semaphore_signal(barrier, inc=1, device_id=at(x, (y + o) % 4), device_id_type=MESH)
    pl.semaphore_signal(barrier, inc=1, device_id=sibling, device_id_type=MESH)

    for load in loads:
        load.wait()
    width = lat_ref.shape[1]
    level = lev_ref[0]
    row = tab_ref[pl.ds(level, 1), :]
    values = lat_ref[...].astype(F32)
    center = values - jnp.mean(values, axis=1, keepdims=True)
    spread = jnp.mean(center * center, axis=1, keepdims=True)
    modulated = center * lax.rsqrt(spread + 1e-06) * (1.0 + row[:, width:]) + row[:, :width]
    modulated = modulated.astype(BF)
    for j in range(NZ):
        xsend[j] = modulated[:, j * BLK:(j + 1) * BLK]
    xr[core, z] = xsend[z]

    def wo_copy(way, t, arrival=False):
        back = t + (1 if arrival else 0)
        slot = (z + NZ - back) % NZ if way == 0 else (z + back) % NZ
        ref = wog.at[core, slot]
        if t == 7:
            ref = wog.at[core, slot, pl.ds(way * (HD // 2), HD // 2)]
        return pltpu.make_async_remote_copy(
            src_ref=ref, dst_ref=ref,
            send_sem=wo_s.at[0], recv_sem=wo_r.at[way, t],
            device_id=along_z(1 if way == 0 else NZ - 1), device_id_type=MESH,
        )

    def wo_sib(side, o):
        ref = wog.at[side, (z + o) % NZ]
        return pltpu.make_async_remote_copy(
            src_ref=ref, dst_ref=ref, send_sem=ws_s.at[0], recv_sem=ws_r.at[0],
            device_id=sibling, device_id_type=MESH,
        )

    def wo_step(t):
        if t > 0:
            for way in range(2):
                wo_copy(way, t - 1, True).wait_recv()
        if t < 8:
            for way in range(2):
                wo_copy(way, t).start()
        if t == 0 or t == 8:
            wo_sib(core, t).start()
        else:
            wo_sib(core, t).start()
            wo_sib(core, NZ - t).start()

    def x_copy(o):
        return pltpu.make_async_remote_copy(
            src_ref=xsend.at[(z + o) % NZ], dst_ref=xr.at[core, z],
            send_sem=xa_s.at[0], recv_sem=xa_r.at[0],
            device_id=along_z(o), device_id_type=MESH,
        )

    pl.semaphore_wait(barrier, 22)
    gw.first()

    for o in FAR_FIRST:
        x_copy(o).start()
    wo_step(0)

    key_span = (lax.broadcasted_iota(jnp.int32, (NT, HD), 0) % HALF) // 8
    query_span = (lax.broadcasted_iota(jnp.int32, (8, NT), 1) % HALF) // 8
    key_order = jnp.zeros((NT, HD), jnp.int32)
    query_order = jnp.zeros((8, NT), jnp.int32)
    for j in range(NZ):
        place = ord_ref[j]
        key_order = jnp.where(key_span == j, place, key_order)
        query_order = jnp.where(query_span == j, place, query_order)
    key_order = jnp.concatenate([key_order, key_order], axis=1)
    mask[...] = jnp.where(key_order <= query_order[0:1, :], 1.0, 0.0)

    take(xr.at[core, pl.ds(0, NZ - 1)], xa_r.at[0])

    def x_sib(slot):
        return pltpu.make_async_remote_copy(
            src_ref=xr.at[slot], dst_ref=xr.at[slot],
            send_sem=sib_s.at[0], recv_sem=sib_r.at[0],
            device_id=sibling, device_id_type=MESH,
        )

    x_sib(core).start()

    def place_of(t, way):
        return (z + 8 - t) % NZ if way == 0 else (z + 8 + t) % NZ

    order_of_use = [place_of(0, 0)]
    for t in range(1, 8):
        order_of_use += [place_of(t, 0), place_of(t, 1)]
    order_of_use.append(z)
    for piece in range(PARTS):
        for block in order_of_use[:FIRST]:
            gw.second(block, piece)

    wo_step(1)
    x_sib(1 - core).wait_recv()
    xin[...] = xr[...].astype(F32).reshape(NT, BLK).astype(BF)

    wo_step(2)

    def rs_copy(way, t, p):
        rows = pl.ds(p * HALF, HALF)
        return pltpu.make_async_remote_copy(
            src_ref=cws.at[way, t, rows], dst_ref=cwr.at[way, t, rows],
            send_sem=rs_s.at[way], recv_sem=rs_r.at[way, t, p],
            device_id=along_z(1 if way == 0 else NZ - 1), device_id_type=MESH,
        )

    for t in range(8):
        if t == 0:
            block = place_of(0, 0)
            gw.use(block)
            cws[0, 0, 0:HALF] = dot(xin[0:HALF], wall[block]).astype(BF)
            rs_copy(0, 0, 0).start()
            cws[1, 0, HALF:NT] = dot(xin[HALF:NT], wall[block]).astype(BF)
            rs_copy(1, 0, 1).start()
        else:
            for way in range(2):
                block = place_of(t, way)
                gw.use(block)
                part[way] = dot(xin[...], wall[block])
            for p in range(2):
                rows = slice(p * HALF, (p + 1) * HALF)
                for way in range(2):
                    total = part[way, rows]
                    if t > 1 or p == way:
                        rs_copy(way, t - 1, p).wait_recv()
                        total = total + cwr[way, t - 1, rows].astype(F32)
                    cws[way, t, rows] = total.astype(BF)
                    rs_copy(way, t, p).start()
        for block in order_of_use[FIRST + 2 * t:FIRST + 2 * t + 2]:
            for piece in range(PARTS):
                gw.second(block, piece)
        if t in WO_AT:
            wo_step(WO_AT[t])
    gw.use(z)
    part[0] = dot(xin[...], wall[z])

    def head_norm(block, gain):
        square = jnp.mean(block * block, axis=-1, keepdims=True)
        return (block * lax.rsqrt(square + 1e-06) * gain).astype(BF)

    def qkv_copy(which, o, p, me):
        ref = (ks, vs, qs)[which].at[me]
        half = pl.ds(p * HALF, HALF)
        ref = ref.at[:, half] if which == 1 else ref.at[half]
        to = at(x, (y + o) % 4) if which < 2 else at((x + o) % 4, y)
        return pltpu.make_async_remote_copy(
            src_ref=ref, dst_ref=ref,
            send_sem=qkv_s.at[0], recv_sem=qkv_r.at[which, o],
            device_id=to, device_id_type=MESH,
        )

    for p in range(2):
        rows = slice(p * HALF, (p + 1) * HALF)
        for way in range(2):
            rs_copy(way, 7, p).wait_recv()
        total = part[0, rows] + cwr[0, 7, rows].astype(F32) + cwr[1, 7, rows].astype(F32)
        total = total.astype(BF).astype(F32)
        ks[y, rows] = head_norm(total[:, HD:2 * HD], kg_ref[...])
        vs[y, :, rows] = jnp.transpose(total[:, 2 * HD:3 * HD]).astype(BF)
        for o in (2, 1, 3):
            for which in range(2):
                qkv_copy(which, o, p, y).start()
        qs[x, rows] = head_norm(total[:, 0:HD], qg_ref[...])
        for o in (2, 1, 3):
            qkv_copy(2, o, p, x).start()
    wo_step(6)
    def nd_copy(which, o):
        src, dst = ((nsend, nrecv), (dsend, drecv))[which]
        return pltpu.make_async_remote_copy(
            src_ref=src.at[o], dst_ref=dst.at[o],
            send_sem=nd_s.at[which], recv_sem=nd_r.at[which, o],
            device_id=at((x + o) % 4, y), device_id_type=MESH,
        )

    def attend(first, j, o):
        queries = qs[(x + o) % 4]
        scores = lax.dot_general(
            ks[j], queries, (((1,), (1,)), ((), ())), preferred_element_type=F32
        ) * HD ** (-0.5)
        probs = jnp.exp(scores) * mask[...]
        low = jnp.sum(probs, axis=0, keepdims=True)
        top = dot(vs[j], probs.astype(BF))
        if not first:
            low = low + lows[o]
            top = top + tops[o]
        return top, low

    def attend_all(first, j):
        for o in range(4):
            tops[o], lows[o] = attend(first, j, o)

    tops[0], lows[0] = attend(True, y, 0)
    for o in (1, 3, 2):
        take(qs.at[(x + 4 - o) % 4], qkv_r.at[2, o])
        tops[4 - o], lows[4 - o] = attend(True, y, 4 - o)
    for o in (1, 3):
        take(ks.at[(y + 4 - o) % 4], qkv_r.at[0, o])
        take(vs.at[(y + 4 - o) % 4], qkv_r.at[1, o])
        attend_all(False, (y + 4 - o) % 4)
        if o == 1:
            wo_step(7)
    take(ks.at[(y + 2) % 4], qkv_r.at[0, 2])
    take(vs.at[(y + 2) % 4], qkv_r.at[1, 2])
    for o in (2, 1, 3):
        top, low = attend(False, (y + 2) % 4, o)
        nsend[o] = top.astype(BF)
        dsend[o] = jnp.broadcast_to(low, (8, NT))
        nd_copy(0, o).start()
        nd_copy(1, o).start()
    top, low = attend(False, (y + 2) % 4, 0)
    wo_step(8)
    for o in (2, 1, 3):
        nd_copy(0, o).wait_recv()
        nd_copy(1, o).wait_recv()
        top = top + nrecv[o].astype(F32)
        low = low + drecv[o][0:1, :]
    asend[...] = jnp.transpose(top / low).reshape(2, NZ, 8, HD).astype(BF)

    home_y, home_x = gw.place(z)
    home = home_y * 4 + home_x
    slot = x * 4 + y

    def aa_copy(side, o):
        way = 0 if side is core else 1
        return pltpu.make_async_remote_copy(
            src_ref=asend.at[side, (z + o) % NZ], dst_ref=brecv.at[core, slot],
            send_sem=aa_s.at[way], recv_sem=aa_r.at[core],
            device_id=((z + o) % NZ, home * 2 + side), device_id_type=MESH,
        )

    for o in FAR_FIRST:
        aa_copy(core, o).start()
        aa_copy(1 - core, o).start()
    aa_copy(1 - core, 0).start()

    @pl.when(home != chip)
    def _():
        aa_copy(core, 0).start()

    @pl.when(home == chip)
    def _():
        brecv[core, slot] = asend[core, z]

    take(wog.at[1 - core], ws_r.at[0])
    take(brecv.at[1 - core], aa_r.at[1 - core])

    @pl.when((home != chip) | (gw.mine != z))
    def _():
        take(brecv.at[core], aa_r.at[core])

    @pl.when((home == chip) & (gw.mine == z))
    def _():
        take(brecv.at[core, pl.ds(0, NZ - 1)], aa_r.at[core])

    rows = [brecv[k].astype(F32).reshape(HALF, HD).astype(BF) for k in range(2)]
    rows = jnp.concatenate(rows, axis=1)

    def sum_copy(phase, half, p, o):
        along_x = (half == 0) == (phase == 0)
        to = at((x + o) % 4, y) if along_x else at(x, (y + o) % 4)
        slot = ((x if along_x else y) + o) % 4
        src, dst, ss, sr = ((ts, tr, t_s, t_r), (us, ur, u_s, u_r))[phase]
        return pltpu.make_async_remote_copy(
            src_ref=src.at[half, p, slot], dst_ref=dst.at[half, p, o],
            send_sem=ss.at[half, p], recv_sem=sr.at[half, p],
            device_id=to, device_id_type=MESH,
        )

    per = WIDE // BLK
    for p in range(PIECES):
        for half in range(2):
            for i in range(per):
                j = half * 8 + p * per + i
                cols = slice(i * BLK, (i + 1) * BLK)
                term = dot(rows, jnp.concatenate([wog[0, j], wog[1, j]], axis=0))
                term = term.reshape(4, 4, 8, BLK)
                for q in range(4):
                    mine = term[q] if half == 0 else term[:, q]
                    ts[half, p, q, :, cols] = mine.reshape(32, BLK).astype(BF)
            for o in (2, 1, 3):
                sum_copy(0, half, p, o).start()
    for p in range(PIECES):
        for half in range(2):
            total = ts[half, p, x if half == 0 else y].astype(F32)
            take(tr.at[half, p, pl.ds(1, 3)], t_r.at[half, p])
            for o in (1, 2, 3):
                total = total + tr[half, p, o].astype(F32)
            us[half, p] = total.reshape(4, 8, WIDE).astype(BF)
            for o in (2, 1, 3):
                sum_copy(1, half, p, o).start()

    take(xsend.at[pl.ds(0, NZ - 1)], xa_s.at[0])
    x_sib(core).wait_send()
    gw.drain()
    take(wall.at[pl.ds(0, 5)], rs_s.at[0])
    take(wall.at[pl.ds(0, 5)], rs_s.at[1])
    take(wall.at[pl.ds(0, 5)], wo_s.at[0])
    take(wog.at[core], ws_s.at[0])
    take(wall.at[pl.ds(0, 2)], qkv_s.at[0])
    take(nsend.at[pl.ds(1, 3)], nd_s.at[0])
    take(dsend.at[pl.ds(1, 3)], nd_s.at[1])
    take(asend.at[1 - core], aa_s.at[1])

    @pl.when(home != chip)
    def _():
        take(asend.at[core], aa_s.at[0])

    @pl.when(home == chip)
    def _():
        take(asend.at[core, pl.ds(0, NZ - 1)], aa_s.at[0])

    for p in range(PIECES):
        for half in range(2):
            take(ts.at[half, p, pl.ds(0, 3)], t_s.at[half, p])

    for p in range(PIECES):
        for half in range(2):
            total = us[half, p, y if half == 0 else x].astype(F32)
            take(ur.at[half, p, pl.ds(1, 3)], u_r.at[half, p])
            for o in (1, 2, 3):
                total = total + ur[half, p, o].astype(F32)
            first = half * 8 * BLK + p * WIDE
            out_ref[:, first:first + WIDE] = total.astype(BF)
    for p in range(PIECES):
        for half in range(2):
            take(us.at[half, p, pl.ds(0, 3)], u_s.at[half, p])


def body(latents, levels, order, level_table, q_gain, k_gain, w_qkv, w_out):
    vmem = pl.BlockSpec(memory_space=pltpu.VMEM)
    smem = pl.BlockSpec(memory_space=pltpu.SMEM)
    hbm = pl.BlockSpec(memory_space=pl.ANY)
    dma = pltpu.SemaphoreType.DMA
    return pl.pallas_call(
        kernel,
        out_shape=jax.ShapeDtypeStruct(latents.shape, BF),
        in_specs=[hbm, smem, smem, hbm, hbm, hbm, hbm, hbm],
        out_specs=vmem,
        scratch_shapes=[
            pltpu.VMEM(latents.shape, BF),
            pltpu.VMEM(level_table.shape, F32),
            pltpu.VMEM((1, HD), F32),
            pltpu.VMEM((1, HD), F32),
            pltpu.VMEM((16, BLK, BLK), BF),
            pltpu.VMEM((NZ, 8, BLK), BF),
            pltpu.VMEM((2, NZ, 8, BLK), BF),
            pltpu.VMEM((NT, BLK), BF),
            pltpu.VMEM((2, NT, BLK), F32),
            pltpu.VMEM((2, 8, NT, BLK), BF),
            pltpu.VMEM((2, 8, NT, BLK), BF),
            pltpu.VMEM((NT, NT), F32),
            pltpu.VMEM((4, NT, HD), BF),
            pltpu.VMEM((4, NT, HD), BF),
            pltpu.VMEM((4, HD, NT), BF),
            pltpu.VMEM((4, HD, NT), BF),
            pltpu.VMEM((4, HD, NT), BF),
            pltpu.VMEM((4, 8, NT), F32),
            pltpu.VMEM((4, 8, NT), F32),
            pltpu.VMEM((4, HD, NT), F32),
            pltpu.VMEM((4, 1, NT), F32),
            pltpu.VMEM((2, NZ, HD, BLK), BF),
            pltpu.VMEM((2, NZ, 8, HD), BF),
            pltpu.VMEM((2, NZ, 8, HD), BF),
            pltpu.VMEM((2, PIECES, 4, 32, WIDE), BF),
            pltpu.VMEM((2, PIECES, 4, 32, WIDE), BF),
            pltpu.VMEM((2, PIECES, 4, 8, WIDE), BF),
            pltpu.VMEM((2, PIECES, 4, 8, WIDE), BF),
            dma((6,)),
            dma((1,)), dma((1,)),
            dma((1,)), dma((1,)),
            dma((2, 2, 3)), dma((2, PARTS, 16)),
            dma((1,)), dma((2, 8)),
            dma((1,)), dma((1,)),
            dma((2,)), dma((2, 8, 2)),
            dma((1,)), dma((3, 4)),
            dma((2,)), dma((2, 4)),
            dma((2,)), dma((2,)),
            dma((2, PIECES)), dma((2, PIECES)),
            dma((2, PIECES)), dma((2, PIECES)),
        ],
        compiler_params=pltpu.CompilerParams(
            collective_id=0, has_side_effects=True, vmem_limit_bytes=60 * 2**20
        ),
        name="spans",
    )(
        latents, levels, order, level_table,
        q_gain.reshape(1, HD), k_gain.reshape(1, HD), w_qkv, w_out,
    )


def solution(mesh):
    placed = (
        P(("span", "seq"), None),
        P("span"),
        P(),
        P(),
        P(),
        P(),
        P("span", "seq"),
        P("seq", "span"),
    )
    return jax.shard_map(
        body, mesh=mesh, in_specs=placed, out_specs=P(("span", "seq"), None), check_vma=False
    )
```

time: 117 us -> 115 us (0.983)
  Pallas kernels: 114 us -> 112 us
    pallas_call x1, Pallas kernels: 114 us -> 112 us  [body(): pl.pallas_call(kernel, out_shape=jax.ShapeDtypeStruct(latents.shape, BF),...]
where the time goes in v4:
time: 115 us; the launch traced here: 114 us
  Pallas kernels  112 us (97%)
  local copies, waits for them, and re-layouts  1.54 us (1%)
    pallas_call x1, Pallas kernels, body(): pl.pallas_call(kernel, out_shape=jax.ShapeDtypeStruct(latents.shape, BF),...  112 us

profile of v4, /device:TPU:1, one launch (start us, length us, event | category | flops | bytes accessed | tf_op | source)
XLA Modules:
  0.0 114.1 jit_solution(14807027831699749529)
XLA Ops:
  0.7 111.9 %spans.1 = bf16[8,6144]{1,0:T(8,128)(2,1)} custom-call(bf16[8,6144]{1,0:T(8,128)(2,1)} %lat_hbm.1, s32[1]{0:T(128)S(6)} %copy.10.lev_ref, s32[16]{0:T(128)} %ord_ref.1, f32[16,12288]{1,0:T(8,128)} %tab_hbm.1, f32[1,128]{1,0:T(1,128)} %bitcast.2, f32[1,128]{1,0:T(1,128)} %bitcast.3, bf16[384,384]{1,0:T(8,128)(2,1)} %w_ref.1, bf16[128,384]{1,0:T(8,128)(2,1)} %wo_ref.1), custom_call_target="tpu_custom_call" | custom-call | tf_op jit(solution)/shard_map/spans/pallas_call | solution.py:483
  112.6 1.5 %copy.11 = bf16[8,6144]{1,0:T(8,128)(2,1)} copy(bf16[8,6144]{1,0:T(8,128)(2,1)} %spans.1) | data formatting | bytes 196608

commit v5 on v4

--- a/solution.py
+++ b/solution.py
@@ -16,7 +16,7 @@
 FAR_FIRST = (8, 7, 9, 6, 10, 5, 11, 4, 12, 3, 13, 2, 14, 1, 15)
 FIRST = 6
 PARTS = 1
-WO_AT = {0: 3, 3: 4, 6: 5}
+WO_AT = {0: 3, 5: 4}
 PIECES = 2
 WIDE = 8 * BLK // PIECES
 
@@ -312,7 +312,7 @@
         qs[x, rows] = head_norm(total[:, 0:HD], qg_ref[...])
         for o in (2, 1, 3):
             qkv_copy(2, o, p, x).start()
-    wo_step(6)
+    wo_step(5)
     def nd_copy(which, o):
         src, dst = ((nsend, nrecv), (dsend, drecv))[which]
         return pltpu.make_async_remote_copy(
@@ -347,7 +347,7 @@
         take(vs.at[(y + 4 - o) % 4], qkv_r.at[1, o])
         attend_all(False, (y + 4 - o) % 4)
         if o == 1:
-            wo_step(7)
+            wo_step(6)
     take(ks.at[(y + 2) % 4], qkv_r.at[0, 2])
     take(vs.at[(y + 2) % 4], qkv_r.at[1, 2])
     for o in (2, 1, 3):
@@ -357,7 +357,7 @@
         nd_copy(0, o).start()
         nd_copy(1, o).start()
     top, low = attend(False, (y + 2) % 4, 0)
-    wo_step(8)
+    wo_step(7)
     for o in (2, 1, 3):
         nd_copy(0, o).wait_recv()
         nd_copy(1, o).wait_recv()
@@ -390,6 +390,7 @@
     def _():
         brecv[core, slot] = asend[core, z]
 
+    wo_step(8)
     take(wog.at[1 - core], ws_r.at[0])
     take(brecv.at[1 - core], aa_r.at[1 - core])
 

time: 115 us -> 114 us (level)
    pallas_call x1, Pallas kernels: 112 us -> 111 us  [body(): pl.pallas_call(kernel, out_shape=jax.ShapeDtypeStruct(latents.shape, BF),...]
where the time goes in v5:
time: 114 us; the launch traced here: 113 us
  Pallas kernels  111 us (97%)
  local copies, waits for them, and re-layouts  1.54 us (1%)
    pallas_call x1, Pallas kernels, body(): pl.pallas_call(kernel, out_shape=jax.ShapeDtypeStruct(latents.shape, BF),...  111 us

profile of v5, /device:TPU:1, one launch (start us, length us, event | category | flops | bytes accessed | tf_op | source)
XLA Modules:
  0.0 112.8 jit_solution(3369134225981487050)
XLA Ops:
  0.7 110.6 %spans.1 = bf16[8,6144]{1,0:T(8,128)(2,1)} custom-call(bf16[8,6144]{1,0:T(8,128)(2,1)} %lat_hbm.1, s32[1]{0:T(128)S(6)} %copy.10.lev_ref, s32[16]{0:T(128)} %ord_ref.1, f32[16,12288]{1,0:T(8,128)} %tab_hbm.1, f32[1,128]{1,0:T(1,128)} %bitcast.2, f32[1,128]{1,0:T(1,128)} %bitcast.3, bf16[384,384]{1,0:T(8,128)(2,1)} %w_ref.1, bf16[128,384]{1,0:T(8,128)(2,1)} %wo_ref.1), custom_call_target="tpu_custom_call" | custom-call | tf_op jit(solution)/shard_map/spans/pallas_call | solution.py:484
  111.3 1.5 %copy.11 = bf16[8,6144]{1,0:T(8,128)(2,1)} copy(bf16[8,6144]{1,0:T(8,128)(2,1)} %spans.1) | data formatting | bytes 196608

commit v6 on v5

--- a/solution.py
+++ b/solution.py
@@ -16,7 +16,7 @@
 FAR_FIRST = (8, 7, 9, 6, 10, 5, 11, 4, 12, 3, 13, 2, 14, 1, 15)
 FIRST = 6
 PARTS = 1
-WO_AT = {0: 3, 5: 4}
+WO_AT = {0: 3, 7: 4}
 PIECES = 2
 WIDE = 8 * BLK // PIECES
 

time: 114 us -> 114 us (level)
  no operation moved by 1% of the time
where the time goes in v6:
time: 114 us; the launch traced here: 113 us
  Pallas kernels  111 us (97%)
  local copies, waits for them, and re-layouts  1.54 us (1%)
    pallas_call x1, Pallas kernels, body(): pl.pallas_call(kernel, out_shape=jax.ShapeDtypeStruct(latents.shape, BF),...  111 us

profile of v6, /device:TPU:1, one launch (start us, length us, event | category | flops | bytes accessed | tf_op | source)
XLA Modules:
  0.0 113.0 jit_solution(12292609335603666849)
XLA Ops:
  0.7 110.8 %spans.1 = bf16[8,6144]{1,0:T(8,128)(2,1)} custom-call(bf16[8,6144]{1,0:T(8,128)(2,1)} %lat_hbm.1, s32[1]{0:T(128)S(6)} %copy.10.lev_ref, s32[16]{0:T(128)} %ord_ref.1, f32[16,12288]{1,0:T(8,128)} %tab_hbm.1, f32[1,128]{1,0:T(1,128)} %bitcast.2, f32[1,128]{1,0:T(1,128)} %bitcast.3, bf16[384,384]{1,0:T(8,128)(2,1)} %w_ref.1, bf16[128,384]{1,0:T(8,128)(2,1)} %wo_ref.1), custom_call_target="tpu_custom_call" | custom-call | tf_op jit(solution)/shard_map/spans/pallas_call | solution.py:484
  111.4 1.5 %copy.11 = bf16[8,6144]{1,0:T(8,128)(2,1)} copy(bf16[8,6144]{1,0:T(8,128)(2,1)} %spans.1) | data formatting | bytes 196608
